TPU v7x, 32 devices: a whole 2x2x4 slice. The times are simulated.
32 devices in a mesh: ctx: 32 (over z, y, x, core), head: 1.
Axes of the slice: x: 2, y: 2, z: 4, core: 2. Of those that a mesh axis runs over, the one named last changes fastest.
Arguments:
- fw_q: bfloat16 [8192, 2048], P('ctx', 'head'), may hold values from -6 to 6
- fw_k: bfloat16 [8192, 2048], P('ctx', 'head'), may hold values from -16 to 16
- fw_v: bfloat16 [8192, 2048], P('ctx', 'head'), may hold values from -6 to 6
- fw_lr: float32 [8192, 4], P('ctx', 'head'), may hold values from 0.1 to 3
- fast_gate: bfloat16 [4, 512, 512], P('head'), may hold values from -0.25 to 0.25
- fast_up: bfloat16 [4, 512, 512], P('head'), may hold values from -0.25 to 0.25
- fast_down: bfloat16 [4, 512, 512], P('head'), may hold values from -0.25 to 0.25
- attn_q: bfloat16 [8192, 2048], P('ctx', 'head'), may hold values from -96 to 96
- attn_k: bfloat16 [8192, 2048], P('ctx', 'head'), may hold values from -10 to 10
- attn_v: bfloat16 [8192, 2048], P('ctx', 'head'), may hold values from -6 to 6
Outputs:
- mixed_out: bfloat16 [8192, 2048], P(('ctx', 'head'))
All inputs are finite; a program needn't handle non-finite values.
Results may differ from a plain program's by a relative error of at most 0.0095.
Values may be sent and summed in bfloat16 or wider, within the bound.
A program may use at most 128 MiB of HBM per device.

v0:
```python
import math

import jax
import jax.numpy as jnp
from jax import lax
from jax.sharding import PartitionSpec as P

SWA_DH = 128
WINDOW = 128
NS_ITERS = 2


linear_coef = 3.4445
square_coef = -4.775
quartic_coef = 2.0315
epsilon = 1e-06


def passed_along(value, axis, steps):
    count = lax.axis_size(axis)
    first, last = (max(0, -steps), min(count, count - steps))
    return lax.ppermute(value, axis, [(source, source + steps) for source in range(first, last)])


def refresh(weight, update):
    initial = weight.astype(jnp.float32)
    stepped = initial - update.astype(jnp.float32)
    old_norm = jnp.sqrt(jnp.sum(initial * initial, axis=-2, keepdims=True) + epsilon)
    new_norm = jnp.sqrt(jnp.sum(stepped * stepped, axis=-2, keepdims=True) + epsilon)
    return (stepped * (old_norm / new_norm)).astype(jnp.bfloat16)


def attend(query_rows, key_window, value_window, device_index):
    row_count = query_rows.shape[0]
    key_count = key_window.shape[0]
    head_total = query_rows.shape[1] // SWA_DH
    query_heads = query_rows.reshape(row_count, head_total, SWA_DH)
    key_heads = key_window.reshape(key_count, head_total, SWA_DH)
    value_heads = value_window.reshape(key_count, head_total, SWA_DH)
    score_scale = 1.0 / math.sqrt(SWA_DH)
    scores = (
        jnp.einsum("qhd,khd->hqk", query_heads, key_heads, preferred_element_type=jnp.float32)
        * score_scale
    )
    query_pos = device_index * row_count + jnp.arange(row_count, dtype=jnp.int32)
    key_pos = device_index * row_count - WINDOW + jnp.arange(key_count, dtype=jnp.int32)
    allowed = (
        (key_pos[None, :] <= query_pos[:, None])
        & (key_pos[None, :] > query_pos[:, None] - WINDOW)
        & (key_pos[None, :] >= 0)
    )
    masked = jnp.where(allowed[None, :, :], scores, -jnp.inf)
    row_peak = jnp.max(masked, axis=-1, keepdims=True)
    exponent = jnp.exp(masked - row_peak)
    row_total = jnp.sum(exponent, axis=-1, keepdims=True)
    weights_bf = (exponent / row_total).astype(jnp.bfloat16)
    result = jnp.einsum("hqk,khd->qhd", weights_bf, value_heads, preferred_element_type=jnp.float32)
    return result.reshape(row_count, head_total * SWA_DH)


def shards(fw_q, fw_k, fw_v, fw_lr, fast_gate, fast_up, fast_down, attn_q, attn_k, attn_v):
    tokens_here = fw_k.shape[0]
    head_count = fast_gate.shape[0]
    head_width = fast_gate.shape[1]
    groups = lax.axis_size("head")
    row_count = tokens_here // groups
    device_index = lax.axis_index("ctx") * groups + lax.axis_index("head")
    tail_pairs = passed_along(jnp.stack([attn_k[-WINDOW:], attn_v[-WINDOW:]]), "ctx", 1)
    extended = jnp.concatenate([tail_pairs, jnp.stack([attn_k, attn_v])], axis=1)
    windows = jnp.stack(
        [
            extended[:, group_index * row_count : group_index * row_count + WINDOW + row_count]
            for group_index in range(groups)
        ]
    )
    query_parts = attn_q.reshape(groups, 1, row_count, attn_q.shape[1])
    got_q, got_kv = (
        lax.all_to_all(query_parts, "head", split_axis=0, concat_axis=3, tiled=True),
        lax.all_to_all(windows, "head", split_axis=0, concat_axis=3, tiled=True),
    )
    query_rows = got_q[0, 0]
    key_window = got_kv[0, 0]
    value_window = got_kv[0, 1]
    key_heads = fw_k.reshape(tokens_here, head_count, head_width)
    value_heads = fw_v.reshape(tokens_here, head_count, head_width)
    query_heads = fw_q.reshape(tokens_here, head_count, head_width)
    pre_gate = jnp.einsum("thi,hij->thj", key_heads, fast_gate, preferred_element_type=jnp.float32)
    pre_up = jnp.einsum("thi,hij->thj", key_heads, fast_up, preferred_element_type=jnp.float32)
    sigmoid_gate = jax.nn.sigmoid(pre_gate)
    activated = pre_gate * sigmoid_gate
    hidden = (activated * pre_up).astype(jnp.bfloat16)
    out_grad = (-(fw_lr[:, :, None] * value_heads.astype(jnp.float32))).astype(jnp.bfloat16)
    grad_down = jnp.einsum("thi,thj->hij", hidden, out_grad, preferred_element_type=jnp.float32)
    hidden_grad = jnp.einsum(
        "thj,hij->thi", out_grad, fast_down, preferred_element_type=jnp.float32
    )
    slope = sigmoid_gate * (1.0 + pre_gate * (1.0 - sigmoid_gate))
    gate_grad = (hidden_grad * pre_up * slope).astype(jnp.bfloat16)
    up_grad = (hidden_grad * activated).astype(jnp.bfloat16)
    grad_gate = jnp.einsum("thi,thj->hij", key_heads, gate_grad, preferred_element_type=jnp.float32)
    grad_up = jnp.einsum("thi,thj->hij", key_heads, up_grad, preferred_element_type=jnp.float32)
    gradients = jnp.stack([grad_gate, grad_up, grad_down], axis=1)
    summed = lax.psum(gradients, "ctx")
    norm_total = jnp.sum(summed * summed, axis=(2, 3))
    iterate = (summed / jnp.sqrt(norm_total + epsilon)[:, :, None, None]).astype(jnp.bfloat16)
    for sweep_index in range(NS_ITERS):
        gram_matrix = jnp.einsum(
            "abij,abkj->abik", iterate, iterate, preferred_element_type=jnp.float32
        ).astype(jnp.bfloat16)
        square = jnp.einsum(
            "abij,abjk->abik", gram_matrix, gram_matrix, preferred_element_type=jnp.float32
        )
        polynomial = (square_coef * gram_matrix.astype(jnp.float32) + quartic_coef * square).astype(
            jnp.bfloat16
        )
        iterate = (
            linear_coef * iterate.astype(jnp.float32)
            + jnp.einsum("abij,abjk->abik", polynomial, iterate, preferred_element_type=jnp.float32)
        ).astype(jnp.bfloat16)
    renewed = refresh(jnp.stack([fast_gate, fast_up, fast_down], axis=1), iterate)
    query_gate = jnp.einsum(
        "thi,hij->thj", query_heads, renewed[:, 0], preferred_element_type=jnp.float32
    )
    query_up = jnp.einsum(
        "thi,hij->thj", query_heads, renewed[:, 1], preferred_element_type=jnp.float32
    )
    query_hidden = (jax.nn.silu(query_gate) * query_up).astype(jnp.bfloat16)
    memory = jnp.einsum(
        "thi,hij->thj", query_hidden, renewed[:, 2], preferred_element_type=jnp.float32
    ).astype(jnp.bfloat16)
    memory = memory.reshape(tokens_here, head_count * head_width)
    memory_rows = lax.all_to_all(memory, "head", split_axis=0, concat_axis=1, tiled=True)
    attended = attend(query_rows, key_window, value_window, device_index)
    return (memory_rows.astype(jnp.float32) + attended).astype(jnp.bfloat16)


def solution(mesh):
    in_specs = (
        P("ctx", "head"),
        P("ctx", "head"),
        P("ctx", "head"),
        P("ctx", "head"),
        P("head", None, None),
        P("head", None, None),
        P("head", None, None),
        P("ctx", "head"),
        P("ctx", "head"),
        P("ctx", "head"),
    )
    out_specs = P(("ctx", "head"), None)
    return jax.shard_map(shards, mesh=mesh, in_specs=in_specs, out_specs=out_specs, check_vma=False)
```

profile of v0, /device:TPU:25, one launch (start us, length us, event | category | flops | bytes accessed | tf_op | source)
XLA Modules:
  0.0 396.0 jit_solution(6909448925248543409)
XLA Ops:
  6.6 2.8 fusion.51
  9.3 2.0 fusion.49
  12.4 3.2 convolution_bitcast_fusion
  15.6 3.1 convolution_bitcast_fusion.2
  18.6 2.9 convolution_bitcast_fusion.1
  21.5 10.7 %pad_maximum_fusion = f32[4,3,512,512]{2,3,0,1:T(8,128)} fusion(f32[4,1,512,512]{2,3,0,1:T(8,128)} %convolution_bitcast_fusion, f32[4,1,512,512]{2,3,0,1:T(8,128)} %convolution_bitcast_fusion.1, f32[4,1,512,512]{2,3,0,1:T(8,128)} %convolution_bitcast_fusion.2), kind=kLoop, calls=%fused_computation.4 | loop fusion | flops 6291456 | bytes 25165824 | tf_op jit(solution)/shard_map/stack | solution.py:102
  34.0 1.9 copy.69
  37.3 3.9 collective-permute-start
  41.3 2.8 copy.42
  44.1 4.2 %copy.43 = bf16[4,512,512]{1,2,0:T(8,128)(2,1)} copy(bf16[4,512,512]{2,1,0:T(8,128)(2,1)} %param.15) | data formatting | bytes 4194304 | tf_op args[5]
  48.3 4.2 %copy.44 = bf16[4,512,512]{1,2,0:T(8,128)(2,1)} copy(bf16[4,512,512]{2,1,0:T(8,128)(2,1)} %param.16) | data formatting | bytes 4194304 | tf_op args[6]
  52.4 2.3 copy.103
  54.9 8.3 %collective-permute-done = bf16[2,128,2048]{1,2,0:T(8,128)(2,1)} collective-permute-done((bf16[2,128,2048]{1,2,0:T(8,128)(2,1)}, bf16[2,128,2048]{1,2,0:T(8,128)(2,1)}, u32[]{:S(2)}, u32[]{:S(2)}) %collective-permute-start) | collective-permute-done | bytes 1048608 | tf_op jit(solution)/shard_map/ppermute | solution.py:22
  63.2 2.4 maximum_bitcast_fusion
  67.0 1.9 fusion.69
  68.9 2.0 fusion.19
  70.9 2.9 copy.76
  73.9 197.9 %all-reduce.2.cloned.1.call-done = f32[4,3,512,512]{2,3,0,1:T(8,128)} async-done(((f32[4,3,512,512]{2,3,0,1:T(8,128)}), f32[4,3,512,512]{2,3,0,1:T(8,128)}) %all-reduce.2.cloned.1.call-update) | async-done | bytes 12582928 | tf_op jit(solution)/shard_map/psum | solution.py:103
  271.7 5.7 %multiply_reduce_fusion.1 = f32[4,3]{0,1:T(4,128)S(1)} fusion(f32[4,3,512,512]{2,3,0,1:T(8,128)} %all-reduce.2.cloned.1.call-done), kind=kLoop, calls=%fused_computation.12 | loop fusion | flops 6291444 | bytes 12582960 | tf_op jit(solution)/shard_map/reduce_sum | solution.py:104
  277.4 9.1 %divide_convert_fusion = bf16[4,3,512,512]{2,3,0,1:T(8,128)(2,1)} fusion(f32[4,3,512,512]{2,3,0,1:T(8,128)} %all-reduce.2.cloned.1.call-done, f32[4,3]{0,1:T(4,128)S(1)} %add_sqrt_fusion), kind=kLoop, calls=%fused_computation.11 | loop fusion | flops 6291456 | bytes 18874416 | tf_op jit(solution)/shard_map/convert_element_type | solution.py:105
  286.6 10.9 %fusion.4 = bf16[4,3,512,512]{3,2,1,0:T(8,128)(2,1)} fusion(bf16[4,3,512,512]{2,3,0,1:T(8,128)(2,1)} %divide_convert_fusion), kind=kOutput, calls=%fused_computation.17 | convolution fusion | flops 3221225472 | bytes 12582912 | tf_op jit(solution)/shard_map/abij,abkj->abik/dot_general | solution.py:107
  297.4 12.6 %add_convert_fusion.3 = bf16[4,3,512,512]{3,2,1,0:T(8,128)(2,1)} fusion(bf16[4,3,512,512]{3,2,1,0:T(8,128)(2,1)} %fusion.4), kind=kOutput, calls=%fused_computation.10 | convolution fusion | flops 3236954112 | bytes 12582912 | tf_op jit(solution)/shard_map/abij,abjk->abik/dot_general | solution.py:110
  310.0 21.4 %add_convert_fusion.2 = bf16[4,3,512,512]{2,3,0,1:T(8,128)(2,1)} fusion(bf16[4,3,512,512]{2,3,0,1:T(8,128)(2,1)} %divide_convert_fusion, bf16[4,3,512,512]{3,2,1,0:T(8,128)(2,1)} %add_convert_fusion.3), kind=kOutput, calls=%fused_computation.9 | convolution fusion | flops 3233808384 | bytes 18874368 | tf_op jit(solution)/shard_map/abij,abjk->abik/dot_general | solution.py:118
  331.5 10.7 %fusion.2 = bf16[4,3,512,512]{3,2,1,0:T(8,128)(2,1)} fusion(bf16[4,3,512,512]{2,3,0,1:T(8,128)(2,1)} %add_convert_fusion.2), kind=kOutput, calls=%fused_computation.15 | convolution fusion | flops 3221225472 | bytes 12582912 | tf_op jit(solution)/shard_map/abij,abkj->abik/dot_general | solution.py:107
  342.2 13.0 %add_convert_fusion.1 = bf16[4,3,512,512]{3,2,1,0:T(8,128)(2,1)} fusion(bf16[4,3,512,512]{3,2,1,0:T(8,128)(2,1)} %fusion.2), kind=kOutput, calls=%fused_computation.8 | convolution fusion | flops 3236954112 | bytes 12582912 | tf_op jit(solution)/shard_map/abij,abjk->abik/dot_general | solution.py:110
  355.2 11.7 %fusion.1 = (f32[4,3,512]{2,0,1:T(4,128)S(1)}, f32[4,3,512]{2,0,1:T(4,128)S(1)}, bf16[4,3,512,512]{2,3,0,1:T(8,128)(2,1)}) fusion(bf16[4,1,512,512]{2,3,0,1:T(8,128)(2,1)} %bitcast.167, bf16[4,1,512,512]{2,3,0,1:T(8,128)(2,1)} %bitcast.165, bf16[4,1,512,512]{2,3,0,1:T(8,128)(2,1)S(1)} %bitcast.163, bf16[4,3,512,512]{2,3,0,1:T(8,128)(2,1)} %add_convert_fusion.2, ...), kind=kOutput, calls=%fused_computation.3 | convolution fusion | flops 3262107648 | bytes 25214976 | tf_op jit(solution)/shard_map/abij,abjk->abik/dot_general | solution.py:118
  367.0 5.4 %multiply_convert_fusion = bf16[4,3,512,512]{2,3,0,1:T(8,128)(2,1)S(1)} fusion(bf16[4,3,512,512]{2,3,0,1:T(8,128)(2,1)} %get-tuple-element.9, f32[4,3,512]{2,0,1:T(4,128)S(1)} %rsqrt_multiply_fusion, bf16[4,1,512,512]{2,3,0,1:T(8,128)(2,1)} %bitcast.168, bf16[4,1,512,512]{2,3,0,1:T(8,128)(2,1)} %bitcast.166, bf16[4,1,512,512]{2,3,0,1:T(8,128)(2,1)S(1)} %bitcast.164), kind=kLoop, calls=%fused_computation.5 | loop fusion | flops 22020096 | bytes 18898944 | tf_op jit(solution)/shard_map/convert_element_type | solution.py:30
  372.4 2.6 copy-done.2
  375.0 2.1 fusion.24
  377.1 6.1 %fusion.40 = f32[4,512,256]{2,1,0:T(8,128)} fusion(bf16[4,3,512,512]{2,3,0,1:T(8,128)(2,1)} %copy-done.2, f32[4,512,256]{1,2,0:T(8,128)} %fusion.24, bf16[256,4,512]{0,2,1:T(8,128)(2,1)} %bitcast.178), kind=kOutput, calls=%fused_computation.69 | convolution fusion | flops 1077936128 | bytes 9437184 | tf_op jit(solution)/shard_map/thi,hij->thj/dot_general | solution.py:128
  383.2 2.9 copy.75
  386.1 2.8 add_convert_fusion.4
  (40 shorter events, 5.8 us)
Async XLA Ops:
  6.5 59.4 %copy-start = (bf16[256,2048]{1,0:T(8,128)(2,1)S(1)}, bf16[256,2048]{1,0:T(8,128)(2,1)}, u32[]{:S(2)}) copy-start(bf16[256,2048]{1,0:T(8,128)(2,1)} %param.17) | copy-start | bytes 3145732
  6.5 2.8 copy-start.3
  6.5 265.2 %all-reduce.2.cloned.1.call-start = ((), (), s32[]{:S(2)}) async-start(), calls=%async_computation | async-start | bytes 25165824 | tf_op jit(solution)/shard_map/psum | solution.py:103
  6.5 4.8 %copy-start.10 = (bf16[256,2048]{1,0:T(8,128)(2,1)S(1)}, bf16[256,2048]{1,0:T(8,128)(2,1)}, u32[]{:S(2)}) copy-start(bf16[256,2048]{1,0:T(8,128)(2,1)} %param.12) | copy-start | bytes 3145732
  6.5 5.0 %copy-start.5 = (bf16[4,512,512]{2,1,0:T(8,128)(2,1)S(1)}, bf16[4,512,512]{2,1,0:T(8,128)(2,1)}, u32[]{:S(2)}) copy-start(bf16[4,512,512]{2,1,0:T(8,128)(2,1)} %param.16) | copy-start | bytes 6291460
  6.6 5.0 %copy-start.12 = (f32[256,4]{0,1:T(4,128)S(1)}, f32[256,4]{0,1:T(4,128)}, u32[]{:S(2)}) copy-start(f32[256,4]{0,1:T(4,128)} %param.13) | copy-start | bytes 12292
  12.4 3.2 copy-start.8
  32.3 1.2 copy-start.11
  34.0 3.3 copy-start.6
  35.9 1.4 copy-start.7
  37.3 25.9 %collective-permute-start = (bf16[2,128,2048]{1,2,0:T(8,128)(2,1)}, bf16[2,128,2048]{1,2,0:T(8,128)(2,1)}, u32[]{:S(2)}, u32[]{:S(2)}) collective-permute-start(bf16[2,128,2048]{1,2,0:T(8,128)(2,1)} %pad_maximum_fusion.2), channel_id=1, source_target_pairs={{0,1},{1,2},{2,3},{3,4},{4,5},{5,6},{6,7},{7,8},{8,9},{9,10},{10,1... | collective-permute-start | bytes 3145736 | tf_op jit(solution)/shard_map/ppermute | solution.py:22
  366.9 8.1 %copy-start.9 = (bf16[256,2048]{0,1:T(8,128)(2,1)S(1)}, bf16[256,2048]{0,1:T(8,128)(2,1)}, u32[]{:S(2)}) copy-start(bf16[256,2048]{0,1:T(8,128)(2,1)} %copy.103) | copy-start | bytes 3145732
  372.4 2.7 copy-start.2
  377.1 9.0 %copy-start.4 = (f32[256,2048]{1,0:T(8,128)S(1)}, f32[256,2048]{1,0:T(8,128)}, u32[]{:S(2)}) copy-start(f32[256,2048]{1,0:T(8,128)} %copy.76) | copy-start | bytes 6291460
  377.1 11.8 %copy-start.1 = (bf16[256,2048]{1,0:T(8,128)(2,1)S(1)}, bf16[256,2048]{1,0:T(8,128)(2,1)}, u32[]{:S(2)}) copy-start(bf16[256,2048]{1,0:T(8,128)(2,1)} %param.17) | copy-start | bytes 3145732
Sparse Core Ops, SparseCore 0:
  32.4 239.2 all-reduce.1
where the time goes:
time: 402 us; the launch traced here: 396 us
  waiting for transfers between devices  206 us (51%)
  matrix products  106 us (26%)
  other arithmetic  39.8 us (10%)
  local copies, waits for them, and re-layouts  26 us (6%)
  between operations  13.8 us (3%)
    psum x1, waiting for transfers between devices, shards(): summed = lax.psum(gradients, 'ctx')  198 us
    dot_general x2, matrix products, shards(): jnp.einsum('abij,abjk->abik', polynomial, iterate, preferred_element_type...  33.2 us
    dot_general x2, matrix products, shards(): jnp.einsum('abij,abjk->abik', gram_matrix, gram_matrix, preferred_element...  25.6 us
    dot_general x2, matrix products, shards(): jnp.einsum('abij,abkj->abik', iterate, iterate, preferred_element_type=jn...  21.6 us
    unnamed x31, local copies, waits for them, and re-layouts  17.4 us
    another operation x1, other arithmetic, shards(): gradients = jnp.stack([grad_gate, grad_up, grad_down], axis=1)  10.7 us
    convert_element_type x1, other arithmetic, shards(): (summed / jnp.sqrt(norm_total + epsilon)[:, :, None, None]).astype(jnp.bf...  9.14 us
    ppermute x1, waiting for transfers between devices, passed_along(): lax.ppermute(value, axis, [(source, source + steps) for source in range(f...  8.32 us
  transfers between devices with their start and end apart: 2, of which 2 were waited for; matrix products, arithmetic and copies ran while one was open for 7% of the time, Pallas kernels for 0%

commit v1 on v0

v1 whole, which is shorter than its diff:
```python
import functools
import math

import jax
import jax.numpy as jnp
from jax import lax
from jax.experimental import pallas as pl
from jax.experimental.pallas import tpu as pltpu
from jax.sharding import PartitionSpec as P

SWA_DH = 128
WINDOW = 128
NS_ITERS = 2
PIECES = 4

linear_coef = 3.4445
square_coef = -4.775
quartic_coef = 2.0315
epsilon = 1e-06

BF16 = jnp.bfloat16
F32 = jnp.float32
MESH = pl.DeviceIdType.MESH


def mat(left, right):
    return jnp.dot(left, right, preferred_element_type=F32)


def mat_tb(left, right):
    return lax.dot_general(left, right, (((1,), (1,)), ((), ())), preferred_element_type=F32)


def mat_ta(left, right):
    return lax.dot_general(left, right, (((0,), (0,)), ((), ())), preferred_element_type=F32)


def sigmoid(value):
    return 1.0 / (1.0 + jnp.exp(-value))


def flip(index, turn, count):
    bit = 1
    while bit < count:
        turn_bit = lax.rem(lax.div(turn, bit), 2)
        index_bit = lax.rem(lax.div(index, bit), 2)
        index = index + turn_bit * (bit - 2 * bit * index_bit)
        bit *= 2
    return index


def kernel(sizes, *refs):
    ctx, heads, chain, rows, width, model, attn = sizes
    fw_q, fw_k, fw_v, fw_lr, w_gate, w_up, w_down = refs[:7]
    refs = refs[7:]
    if attn:
        attn_q, attn_k, attn_v = refs[:3]
        refs = refs[3:]
    out = refs[0]
    (keys, grads, queries, grad_out, answers, returned, values, rates, weights, renewed,
     total, core_out, core_in, chain_out, chain_in, iter_a, iter_b, gram, poly,
     local_sem, key_s, key_r, og_s, og_r, q_s, q_r, ans_s, ans_r,
     core_s, core_r, chain_s, chain_r, cast_s, cast_r, side_s, side_r) = refs[1:37]
    if attn:
        q_rows, key_window, value_window, attended, halo_s, halo_r = refs[37:]

    me = lax.axis_index("ctx")
    core = lax.rem(me, 2)
    head = lax.rem(lax.div(me, 2), heads)
    z = lax.div(me, 2 * heads)
    mate = me + 1 - 2 * core
    step = 2 * heads
    piece_rows = width // PIECES

    def partner(turn):
        return me + 2 * (flip(head, turn, heads) - head)

    def columns(index):
        return pl.ds(pl.multiple_of(index * width, 128), width)

    def remote(src, dst, send, recv, device):
        return pltpu.make_async_remote_copy(
            src_ref=src, dst_ref=dst, send_sem=send, recv_sem=recv,
            device_id={"ctx": device}, device_id_type=MESH,
        )

    local = [
        pltpu.make_async_copy(fw_v, values, local_sem.at[0]),
        pltpu.make_async_copy(fw_lr, rates, local_sem.at[1]),
        pltpu.make_async_copy(fw_k.at[:, columns(head)], keys.at[head], local_sem.at[2]),
        pltpu.make_async_copy(w_gate.at[head], weights.at[0], local_sem.at[3]),
        pltpu.make_async_copy(w_up.at[head], weights.at[1], local_sem.at[4]),
        pltpu.make_async_copy(w_down.at[head], weights.at[2], local_sem.at[5]),
        pltpu.make_async_copy(fw_q.at[:, columns(head)], queries.at[head], local_sem.at[6]),
    ]
    if attn:
        local += [
            pltpu.make_async_copy(attn_q, q_rows, local_sem.at[7]),
            pltpu.make_async_copy(attn_k, key_window.at[pl.ds(WINDOW, rows)], local_sem.at[8]),
            pltpu.make_async_copy(attn_v, value_window.at[pl.ds(WINDOW, rows)], local_sem.at[9]),
        ]
    for copy in local:
        copy.start()

    barrier = pltpu.get_barrier_semaphore()

    def greet(device):
        pl.semaphore_signal(barrier, inc=1, device_id={"ctx": device}, device_id_type=MESH)

    for turn in range(1, heads):
        greet(partner(turn))
    greet(mate)
    expected = jnp.int32(heads)
    checks = [(z > 0, me - step), (z < chain - 1, me + step)]
    if attn:
        checks += [(me > 0, me - 1), (me < ctx - 1, me + 1)]
    for there, device in checks:
        pl.when(there)(functools.partial(greet, device))
        expected = expected + there.astype(jnp.int32)
    pl.semaphore_wait(barrier, expected)

    def key_copy(turn):
        other = flip(head, turn, heads)
        return remote(fw_k.at[:, columns(other)], keys.at[head], key_s.at[turn], key_r.at[turn],
                      partner(turn))

    def og_copy(turn):
        other = flip(head, turn, heads)
        return remote(grad_out.at[other], grads.at[head], og_s.at[turn], og_r.at[turn],
                      partner(turn))

    def query_copy(turn):
        other = flip(head, turn, heads)
        return remote(fw_q.at[:, columns(other)], queries.at[head], q_s.at[turn], q_r.at[turn],
                      partner(turn))

    def answer_copy(turn):
        return remote(answers.at[turn], returned.at[head], ans_s.at[turn], ans_r.at[turn],
                      partner(turn))

    for turn in range(1, heads):
        key_copy(turn).start()
    local[0].wait()
    local[1].wait()
    for index in range(heads):
        cols = slice(index * width, (index + 1) * width)
        grad_out[index] = (-(rates[:, index : index + 1] * values[:, cols].astype(F32))).astype(BF16)
    for turn in range(1, heads):
        og_copy(turn).start()

    def accumulate(key_ref, og_ref, first):
        key_rows = key_ref[...]
        og = og_ref[...]
        pre_gate = mat(key_rows, weights[0])
        pre_up = mat(key_rows, weights[1])
        hidden_grad = mat_tb(og, weights[2])
        sig = sigmoid(pre_gate)
        activated = pre_gate * sig
        hidden = (activated * pre_up).astype(BF16)
        gate_grad = (hidden_grad * pre_up * (sig * (1.0 + pre_gate * (1.0 - sig)))).astype(BF16)
        up_grad = (hidden_grad * activated).astype(BF16)
        for index, (left, right) in enumerate(
            ((key_rows, gate_grad), (key_rows, up_grad), (hidden, og))
        ):
            if first:
                total[index] = mat_ta(left, right)
            else:
                total[index] += mat_ta(left, right)

    for index in range(2, 6):
        local[index].wait()
    accumulate(keys.at[head], grad_out.at[head], True)

    if attn:
        score_scale = 1.0 / math.sqrt(SWA_DH)
        swa_heads = model // SWA_DH
        row_id = lax.broadcasted_iota(jnp.int32, (WINDOW, 2 * WINDOW), 0)
        col_id = lax.broadcasted_iota(jnp.int32, (WINDOW, 2 * WINDOW), 1)

        def attend(block):
            allowed = (col_id > row_id) & (col_id <= row_id + WINDOW)
            if block == 0:
                allowed = allowed & (col_id >= jnp.where(me == 0, WINDOW, 0))
            here = slice(block * WINDOW, (block + 1) * WINDOW)
            there = slice(block * WINDOW, (block + 2) * WINDOW)

            def one(index, carry):
                cols = pl.ds(pl.multiple_of(index * SWA_DH, SWA_DH), SWA_DH)
                scores = mat_tb(q_rows[here, cols], key_window[there, cols]) * score_scale
                masked = jnp.where(allowed, scores, -jnp.inf)
                peak = jnp.max(masked, axis=-1, keepdims=True)
                exponent = jnp.exp(masked - peak)
                probs = (exponent / jnp.sum(exponent, axis=-1, keepdims=True)).astype(BF16)
                attended[here, cols] = mat(probs, value_window[there, cols])
                return carry

            lax.fori_loop(0, swa_heads, one, 0, unroll=4 if swa_heads % 4 == 0 else 1)

        for index in range(7, 10):
            local[index].wait()
        for block in range(1, rows // WINDOW):
            attend(block)

    def gather_turn(turn, carry):
        key_copy(turn).wait_recv()
        og_copy(turn).wait_recv()
        other = flip(head, turn, heads)
        accumulate(keys.at[other], grads.at[other], False)
        return carry

    lax.fori_loop(1, heads, gather_turn, 0)

    def home(matrix):
        return jnp.minimum(matrix, 1)

    def root(matrix):
        return jnp.where(matrix == 1, chain - 1, 0)

    def toward(matrix):
        return jnp.where(matrix == 1, 1, -1)

    def part(piece):
        return pl.ds(piece * piece_rows, piece_rows)

    def core_copy(matrix, piece):
        return remote(core_out.at[matrix, part(piece)], core_in.at[matrix, part(piece)],
                      core_s.at[matrix, piece], core_r.at[matrix, piece], mate)

    def chain_copy(matrix, piece):
        return remote(chain_out.at[matrix, part(piece)], chain_in.at[matrix, part(piece)],
                      chain_s.at[matrix, piece], chain_r.at[matrix, piece],
                      me + step * toward(matrix))

    def cast_copy(matrix, piece):
        return remote(renewed.at[matrix, part(piece)], renewed.at[matrix, part(piece)],
                      cast_s.at[matrix, piece], cast_r.at[matrix, piece],
                      me - step * toward(matrix))

    def side_copy(matrix, piece):
        return remote(renewed.at[matrix, part(piece)], renewed.at[matrix, part(piece)],
                      side_s.at[matrix, piece], side_r.at[matrix, piece], mate)

    def starts(matrix):
        return z == chain - 1 - root(matrix)

    def ends(matrix):
        return z == root(matrix)

    for piece in range(PIECES):
        for matrix in range(3):
            @pl.when(core != min(matrix, 1))
            def _():
                core_out[matrix, part(piece)] = total[matrix, part(piece)].astype(BF16)
                core_copy(matrix, piece).start()

    for turn in range(1, heads):
        query_copy(turn).start()

    if attn:
        def halo_copy(which):
            source = (attn_k, attn_v)[which]
            target = (key_window, value_window)[which]
            return remote(source.at[pl.ds(rows - WINDOW, WINDOW)], target.at[pl.ds(0, WINDOW)],
                          halo_s.at[which], halo_r.at[which], me + 1)

        @pl.when(me < ctx - 1)
        def _():
            halo_copy(0).start()
            halo_copy(1).start()

        @pl.when(me == 0)
        def _():
            key_window[0:WINDOW] = jnp.zeros((WINDOW, model), BF16)
            value_window[0:WINDOW] = jnp.zeros((WINDOW, model), BF16)

    def sum_piece(matrix, piece, has_input):
        core_copy(matrix, piece).wait_recv()
        summed = total[matrix, part(piece)] + core_in[matrix, part(piece)].astype(F32)
        if has_input:
            chain_copy(matrix, piece).wait_recv()
            summed = summed + chain_in[matrix, part(piece)].astype(F32)

        @pl.when(ends(matrix))
        def _():
            total[matrix, part(piece)] = summed

        @pl.when(jnp.logical_not(ends(matrix)))
        def _():
            chain_out[matrix, part(piece)] = summed.astype(BF16)
            chain_copy(matrix, piece).start()

    def start_chain(matrix, carry):
        @pl.when((core == home(matrix)) & starts(matrix))
        def _():
            for piece in range(PIECES):
                sum_piece(matrix, piece, False)
        return carry

    lax.fori_loop(0, 3, start_chain, 0)

    order = [(0, 0)]
    for piece in range(1, PIECES):
        order += [(0, piece), (1, piece - 1)]
    order += [(1, PIECES - 1)]

    def sum_rest(matrix, piece):
        @pl.when(jnp.logical_not(starts(matrix)))
        def _():
            sum_piece(matrix, piece, True)

    @pl.when(core == 0)
    def _():
        for piece in range(PIECES):
            sum_rest(0, piece)

    near_sum = jnp.where(2 * z < chain, 1, 2)

    @pl.when(core == 1)
    def _():
        for which, piece in order:
            sum_rest(near_sum if which == 0 else 3 - near_sum, piece)

    half = min(256, width)
    tiles = width // half

    def tile_loop(body):
        def run(index, carry):
            body(pl.ds(pl.multiple_of(index * half, half), half))
            return carry
        lax.fori_loop(0, tiles, run, 0)

    def renew(matrix):
        gradient = total[matrix]
        norm = jnp.sqrt(jnp.sum(gradient * gradient) + epsilon)
        iter_a[...] = (gradient / norm).astype(BF16)
        source, target = iter_a, iter_b
        for _ in range(NS_ITERS):
            def gram_rows(here, source=source):
                gram[here, :] = mat_tb(source[here, :], source[...]).astype(BF16)

            def poly_rows(here):
                mine = gram[here, :]
                square = mat(mine, gram[...])
                poly[here, :] = (square_coef * mine.astype(F32) + quartic_coef * square).astype(BF16)

            def next_rows(here, source=source, target=target):
                target[here, :] = (
                    linear_coef * source[here, :].astype(F32) + mat(poly[here, :], source[...])
                ).astype(BF16)

            tile_loop(gram_rows)
            tile_loop(poly_rows)
            tile_loop(next_rows)
            source, target = target, source
        initial = weights[matrix].astype(F32)
        stepped = initial - source[...].astype(F32)
        old_norm = jnp.sqrt(jnp.sum(initial * initial, axis=0, keepdims=True) + epsilon)
        new_norm = jnp.sqrt(jnp.sum(stepped * stepped, axis=0, keepdims=True) + epsilon)
        renewed[matrix] = (stepped * (old_norm / new_norm)).astype(BF16)

    def pass_on(matrix, piece):
        @pl.when(jnp.logical_not(starts(matrix)))
        def _():
            cast_copy(matrix, piece).start()

        side_copy(matrix, piece).start()

    def renew_here(matrix, carry):
        @pl.when((core == home(matrix)) & ends(matrix))
        def _():
            renew(matrix)
            for piece in range(PIECES):
                pass_on(matrix, piece)
        return carry

    lax.fori_loop(0, 3, renew_here, 0)

    if attn:
        @pl.when(me > 0)
        def _():
            halo_copy(0).wait_recv()
            halo_copy(1).wait_recv()
        attend(0)

    def forward(matrix, piece):
        @pl.when(jnp.logical_not(ends(matrix)))
        def _():
            cast_copy(matrix, piece).wait_recv()
            pass_on(matrix, piece)

    @pl.when(core == 0)
    def _():
        for piece in range(PIECES):
            forward(0, piece)

    @pl.when(core == 1)
    def _():
        for which, piece in order:
            forward(3 - near_sum if which == 0 else near_sum, piece)

    for matrix in range(3):
        @pl.when(core != min(matrix, 1))
        def _():
            for piece in range(PIECES):
                side_copy(matrix, piece).wait_recv()

    def answer(query_ref):
        query_rows = query_ref[...]
        pre_gate = mat(query_rows, renewed[0])
        pre_up = mat(query_rows, renewed[1])
        hidden = (pre_gate * sigmoid(pre_gate) * pre_up).astype(BF16)
        return mat(hidden, renewed[2]).astype(BF16)

    def answer_turn(turn, carry):
        query_copy(turn).wait_recv()
        answers[turn] = answer(queries.at[flip(head, turn, heads)])
        answer_copy(turn).start()
        return carry

    lax.fori_loop(1, heads, answer_turn, 0)
    local[6].wait()
    answers[0] = answer(queries.at[head])

    def finish(value, index):
        if attn:
            value = (value.astype(F32) + attended[:, columns(index)]).astype(BF16)
        out[:, columns(index)] = value

    finish(answers[0], head)
    for turn in range(1, heads):
        answer_copy(turn).wait_recv()
        other = flip(head, turn, heads)
        finish(returned[other], other)

    for turn in range(1, heads):
        key_copy(turn).wait_send()
        og_copy(turn).wait_send()
        query_copy(turn).wait_send()
        answer_copy(turn).wait_send()
    if attn:
        @pl.when(me < ctx - 1)
        def _():
            halo_copy(0).wait_send()
            halo_copy(1).wait_send()
    for matrix in range(3):
        @pl.when(core != min(matrix, 1))
        def _():
            for piece in range(PIECES):
                core_copy(matrix, piece).wait_send()

        @pl.when(core == min(matrix, 1))
        def _():
            for piece in range(PIECES):
                side_copy(matrix, piece).wait_send()

            @pl.when(jnp.logical_not(ends(matrix)))
            def _():
                for piece in range(PIECES):
                    chain_copy(matrix, piece).wait_send()

            @pl.when(jnp.logical_not(starts(matrix)))
            def _():
                for piece in range(PIECES):
                    cast_copy(matrix, piece).wait_send()


def memory_call(attn, *arrays):
    rows = arrays[0].shape[0]
    heads, width = arrays[4].shape[:2]
    ctx = lax.axis_size("ctx")
    chain = ctx // (2 * heads)
    model = arrays[0].shape[1]
    swa_model = arrays[-1].shape[1]
    square = (width, width)
    tokens = (heads, rows, width)
    dma = pltpu.SemaphoreType.DMA
    scratch = [pltpu.VMEM(tokens, BF16)] * 6
    scratch += [
        pltpu.VMEM((rows, model), BF16),
        pltpu.VMEM((rows, heads), F32),
        pltpu.VMEM((3,) + square, BF16),
        pltpu.VMEM((3,) + square, BF16),
        pltpu.VMEM((3,) + square, F32),
    ]
    scratch += [pltpu.VMEM((3,) + square, BF16)] * 4
    scratch += [pltpu.VMEM(square, BF16)] * 4
    scratch += [dma((10,))]
    scratch += [dma((heads,))] * 8
    scratch += [dma((3, PIECES))] * 8
    if attn:
        scratch += [
            pltpu.VMEM((rows, swa_model), BF16),
            pltpu.VMEM((rows + WINDOW, swa_model), BF16),
            pltpu.VMEM((rows + WINDOW, swa_model), BF16),
            pltpu.VMEM((rows, swa_model), F32),
            dma((2,)),
            dma((2,)),
        ]
    sizes = (ctx, heads, chain, rows, width, swa_model, attn)
    flops = 2 * rows * heads * width * width * 9 + 6 * NS_ITERS * width**3
    return pl.pallas_call(
        functools.partial(kernel, sizes),
        out_shape=jax.ShapeDtypeStruct((rows, model), BF16),
        in_specs=[pl.BlockSpec(memory_space=pl.ANY)] * len(arrays),
        out_specs=pl.BlockSpec(memory_space=pltpu.VMEM),
        scratch_shapes=scratch,
        cost_estimate=pl.CostEstimate(
            flops=flops, bytes_accessed=8 * rows * model * 2, transcendentals=rows * model
        ),
        compiler_params=pltpu.CompilerParams(
            collective_id=0, has_side_effects=True, vmem_limit_bytes=50 * 1024 * 1024
        ),
    )(*arrays)


def passed_along(value, axis, steps):
    count = lax.axis_size(axis)
    first, last = (max(0, -steps), min(count, count - steps))
    return lax.ppermute(value, axis, [(source, source + steps) for source in range(first, last)])


def attend(query_rows, key_window, value_window, device_index):
    row_count = query_rows.shape[0]
    key_count = key_window.shape[0]
    head_total = query_rows.shape[1] // SWA_DH
    query_heads = query_rows.reshape(row_count, head_total, SWA_DH)
    key_heads = key_window.reshape(key_count, head_total, SWA_DH)
    value_heads = value_window.reshape(key_count, head_total, SWA_DH)
    score_scale = 1.0 / math.sqrt(SWA_DH)
    scores = (
        jnp.einsum("qhd,khd->hqk", query_heads, key_heads, preferred_element_type=jnp.float32)
        * score_scale
    )
    query_pos = device_index * row_count + jnp.arange(row_count, dtype=jnp.int32)
    key_pos = device_index * row_count - WINDOW + jnp.arange(key_count, dtype=jnp.int32)
    allowed = (
        (key_pos[None, :] <= query_pos[:, None])
        & (key_pos[None, :] > query_pos[:, None] - WINDOW)
        & (key_pos[None, :] >= 0)
    )
    masked = jnp.where(allowed[None, :, :], scores, -jnp.inf)
    row_peak = jnp.max(masked, axis=-1, keepdims=True)
    exponent = jnp.exp(masked - row_peak)
    row_total = jnp.sum(exponent, axis=-1, keepdims=True)
    weights_bf = (exponent / row_total).astype(jnp.bfloat16)
    result = jnp.einsum("hqk,khd->qhd", weights_bf, value_heads, preferred_element_type=jnp.float32)
    return result.reshape(row_count, head_total * SWA_DH)


def shards(fw_q, fw_k, fw_v, fw_lr, fast_gate, fast_up, fast_down, attn_q, attn_k, attn_v):
    fast = (fw_q, fw_k, fw_v, fw_lr, fast_gate, fast_up, fast_down)
    groups = lax.axis_size("head")
    if groups == 1:
        return memory_call(True, *fast, attn_q, attn_k, attn_v)
    tokens_here = fw_k.shape[0]
    row_count = tokens_here // groups
    device_index = lax.axis_index("ctx") * groups + lax.axis_index("head")
    tail_pairs = passed_along(jnp.stack([attn_k[-WINDOW:], attn_v[-WINDOW:]]), "ctx", 1)
    extended = jnp.concatenate([tail_pairs, jnp.stack([attn_k, attn_v])], axis=1)
    windows = jnp.stack(
        [
            extended[:, group_index * row_count : group_index * row_count + WINDOW + row_count]
            for group_index in range(groups)
        ]
    )
    query_parts = attn_q.reshape(groups, 1, row_count, attn_q.shape[1])
    got_q, got_kv = (
        lax.all_to_all(query_parts, "head", split_axis=0, concat_axis=3, tiled=True),
        lax.all_to_all(windows, "head", split_axis=0, concat_axis=3, tiled=True),
    )
    memory = memory_call(False, *fast)
    memory_rows = lax.all_to_all(memory, "head", split_axis=0, concat_axis=1, tiled=True)
    attended = attend(got_q[0, 0], got_kv[0, 0], got_kv[0, 1], device_index)
    return (memory_rows.astype(jnp.float32) + attended).astype(jnp.bfloat16)


def solution(mesh):
    in_specs = (
        P("ctx", "head"),
        P("ctx", "head"),
        P("ctx", "head"),
        P("ctx", "head"),
        P("head", None, None),
        P("head", None, None),
        P("head", None, None),
        P("ctx", "head"),
        P("ctx", "head"),
        P("ctx", "head"),
    )
    out_specs = P(("ctx", "head"), None)
    return jax.shard_map(shards, mesh=mesh, in_specs=in_specs, out_specs=out_specs, check_vma=False)
```

time: 402 us -> 101 us (0.25); the launches traced: 396 us -> 100 us
  waiting for transfers between devices: 206 us -> 0 us
  matrix products: 106 us -> 0 us
  Pallas kernels: 0 us -> 96.2 us
  other arithmetic: 39.8 us -> 0 us
  local copies, waits for them, and re-layouts: 26 us -> 4.23 us
  between operations: 13.8 us -> 0.03 us
    psum x1 -> x0, waiting for transfers between devices: 198 us -> none  [shards(): summed = lax.psum(gradients, 'ctx')]
    dot_general x16 -> x0, matrix products: 106 us -> none  [the longest x2 33.2 us: shards(): jnp.einsum('abij,abjk->abik', polynomial, iterate, preferred_element_type...]
    pallas_call x0 -> x1, Pallas kernels: none -> 96.2 us  [memory_call(): pl.pallas_call(functools.partial(kernel, sizes), out_shape=jax.ShapeDtype...]
    convert_element_type x4 -> x0, other arithmetic: 17.6 us -> none  [the longest x1 9.14 us: shards(): (summed / jnp.sqrt(norm_total + epsilon)[:, :, None, None]).astype(jnp.bf...]
    another operation x3 -> x0, other arithmetic: 14.4 us -> none  [the longest x1 10.7 us: shards(): gradients = jnp.stack([grad_gate, grad_up, grad_down], axis=1)]
    unnamed x31 -> x6, local copies, waits for them, and re-layouts: 17.4 us -> 4.23 us
    ppermute x1 -> x0, waiting for transfers between devices: 8.32 us -> none  [passed_along(): lax.ppermute(value, axis, [(source, source + steps) for source in range(f...]
    reduce_sum x1 -> x0, other arithmetic: 5.67 us -> none  [shards(): norm_total = jnp.sum(summed * summed, axis=(2, 3))]
  transfers between devices with their start and end apart: 2 -> 0, of which waited for: 2 -> 0; matrix products, arithmetic and copies ran while one was open for 7% -> 0% of each run, Pallas kernels for 0% -> 0%
where the time goes in v1:
time: 101 us; the launch traced here: 100 us
  Pallas kernels  96.2 us (95%)
  local copies, waits for them, and re-layouts  4.23 us (4%)
    pallas_call x1, Pallas kernels, memory_call(): pl.pallas_call(functools.partial(kernel, sizes), out_shape=jax.ShapeDtype...  96.2 us
    unnamed x6, local copies, waits for them, and re-layouts  4.23 us

profile of v1, /device:TPU:25, one launch (start us, length us, event | category | flops | bytes accessed | tf_op | source)
XLA Modules:
  0.0 100.4 jit_solution(7633306288367093002)
XLA Ops:
  0.0 0.8 copy.11.refs_3_
  0.8 0.0 copy-start
  0.8 1.2 %copy-done = bf16[256,2048]{1,0:T(8,128)(2,1)S(1)} copy-done((bf16[256,2048]{1,0:T(8,128)(2,1)S(1)}, bf16[256,2048]{1,0:T(8,128)(2,1)}, u32[]{:S(2)}) %copy-start) | copy-done | bytes 1048600
  2.1 0.0 copy-start.1
  2.1 1.2 %copy-done.1 = bf16[256,2048]{1,0:T(8,128)(2,1)S(1)} copy-done((bf16[256,2048]{1,0:T(8,128)(2,1)S(1)}, bf16[256,2048]{1,0:T(8,128)(2,1)}, u32[]{:S(2)}) %copy-start.1) | copy-done | bytes 1048600
  3.3 96.2 %shard_map.100 = bf16[256,2048]{1,0:T(8,128)(2,1)S(1)} custom-call(bf16[256,2048]{1,0:T(8,128)(2,1)S(1)} %copy-done, bf16[256,2048]{1,0:T(8,128)(2,1)S(1)} %copy-done.1, bf16[256,2048]{1,0:T(8,128)(2,1)} %refs_2_.1, f32[256,4]{1,0:T(8,128)S(1)} %copy.11.refs_3_, bf16[4,512,512]{2,1,0:T(8,128)(2,1)} %refs_4_.1, bf16[4,512,512]{2,1,0:T(8,128)(2,1)} %refs_5_.1, ...), custom_call_target="tpu_custom_call" | custom-call | flops 6442450944 | bytes 8388608 | tf_op jit(solution)/shard_map/pallas_call | solution.py:501
  99.4 1.0 copy.13
Async XLA Ops:
  0.8 1.2 %copy-start = (bf16[256,2048]{1,0:T(8,128)(2,1)S(1)}, bf16[256,2048]{1,0:T(8,128)(2,1)}, u32[]{:S(2)}) copy-start(bf16[256,2048]{1,0:T(8,128)(2,1)} %refs_0_.1) | copy-start | bytes 3145732
  2.1 1.2 %copy-start.1 = (bf16[256,2048]{1,0:T(8,128)(2,1)S(1)}, bf16[256,2048]{1,0:T(8,128)(2,1)}, u32[]{:S(2)}) copy-start(bf16[256,2048]{1,0:T(8,128)(2,1)} %refs_1_.1) | copy-start | bytes 3145732

commit v2 on v1

--- a/solution.py
+++ b/solution.py
@@ -57,12 +57,12 @@
         attn_q, attn_k, attn_v = refs[:3]
         refs = refs[3:]
     out = refs[0]
-    (keys, grads, queries, grad_out, answers, returned, values, rates, weights, renewed,
+    (keys, grads, queries, grad_out, answers, returned, hiddens, values, rates, weights, renewed,
      total, core_out, core_in, chain_out, chain_in, iter_a, iter_b, gram, poly,
      local_sem, key_s, key_r, og_s, og_r, q_s, q_r, ans_s, ans_r,
-     core_s, core_r, chain_s, chain_r, cast_s, cast_r, side_s, side_r) = refs[1:37]
-    if attn:
-        q_rows, key_window, value_window, attended, halo_s, halo_r = refs[37:]
+     core_s, core_r, chain_s, chain_r, cast_s, cast_r, side_s, side_r) = refs[1:38]
+    if attn:
+        q_rows, key_window, value_window, attended, relay, halo_s, halo_r, relay_s, relay_r = refs[38:]
 
     me = lax.axis_index("ctx")
     core = lax.rem(me, 2)
@@ -71,6 +71,14 @@
     mate = me + 1 - 2 * core
     step = 2 * heads
     piece_rows = width // PIECES
+    first = lax.rem(me, step) == 0
+    last = lax.rem(me, step) == step - 1
+    halo_to = me + 1 - jnp.where(last, step, 0)
+    halo_from = me - 1 + jnp.where(first, step, 0)
+    halo_sends = jnp.logical_not(last) | (z > 0)
+    halo_comes = jnp.logical_not(first) | (z > 0)
+    relay_sends = last & (z < chain - 1)
+    relay_comes = last & (z > 0)
 
     def partner(turn):
         return me + 2 * (flip(head, turn, heads) - head)
@@ -113,7 +121,7 @@
     expected = jnp.int32(heads)
     checks = [(z > 0, me - step), (z < chain - 1, me + step)]
     if attn:
-        checks += [(me > 0, me - 1), (me < ctx - 1, me + 1)]
+        checks += [(halo_comes, halo_from), (halo_sends, halo_to)]
     for there, device in checks:
         pl.when(there)(functools.partial(greet, device))
         expected = expected + there.astype(jnp.int32)
@@ -134,17 +142,35 @@
         return remote(fw_q.at[:, columns(other)], queries.at[head], q_s.at[turn], q_r.at[turn],
                       partner(turn))
 
-    def answer_copy(turn):
-        return remote(answers.at[turn], returned.at[head], ans_s.at[turn], ans_r.at[turn],
-                      partner(turn))
+    def half_columns(part_index):
+        return pl.ds(part_index * (width // 2), width // 2)
+
+    def answer_copy(turn, part_index):
+        cols = half_columns(part_index)
+        return remote(answers.at[turn, :, cols], returned.at[head, :, cols],
+                      ans_s.at[turn, part_index], ans_r.at[turn, part_index], partner(turn))
 
     for turn in range(1, heads):
         key_copy(turn).start()
+    if attn:
+        def relay_copy(which):
+            source = (attn_k, attn_v)[which]
+            return remote(source.at[pl.ds(rows - WINDOW, WINDOW)], relay.at[which],
+                          relay_s.at[which], relay_r.at[which], me + step)
+
+        @pl.when(relay_sends)
+        def _():
+            relay_copy(0).start()
+            relay_copy(1).start()
+
     local[0].wait()
     local[1].wait()
+    rate_columns = jnp.transpose(rates[...])
     for index in range(heads):
         cols = slice(index * width, (index + 1) * width)
-        grad_out[index] = (-(rates[:, index : index + 1] * values[:, cols].astype(F32))).astype(BF16)
+        grad_out[index] = (
+            -(rate_columns[:, index : index + 1] * values[:, cols].astype(F32))
+        ).astype(BF16)
     for turn in range(1, heads):
         og_copy(turn).start()
 
@@ -211,7 +237,7 @@
     lax.fori_loop(1, heads, gather_turn, 0)
 
     def home(matrix):
-        return jnp.minimum(matrix, 1)
+        return lax.rem(matrix, 2)
 
     def root(matrix):
         return jnp.where(matrix == 1, chain - 1, 0)
@@ -231,14 +257,17 @@
                       chain_s.at[matrix, piece], chain_r.at[matrix, piece],
                       me + step * toward(matrix))
 
+    def piece_columns(piece):
+        return pl.ds(piece * piece_rows, piece_rows)
+
     def cast_copy(matrix, piece):
-        return remote(renewed.at[matrix, part(piece)], renewed.at[matrix, part(piece)],
-                      cast_s.at[matrix, piece], cast_r.at[matrix, piece],
+        here = renewed.at[matrix, :, piece_columns(piece)]
+        return remote(here, here, cast_s.at[matrix, piece], cast_r.at[matrix, piece],
                       me - step * toward(matrix))
 
     def side_copy(matrix, piece):
-        return remote(renewed.at[matrix, part(piece)], renewed.at[matrix, part(piece)],
-                      side_s.at[matrix, piece], side_r.at[matrix, piece], mate)
+        here = renewed.at[matrix, :, piece_columns(piece)]
+        return remote(here, here, side_s.at[matrix, piece], side_r.at[matrix, piece], mate)
 
     def starts(matrix):
         return z == chain - 1 - root(matrix)
@@ -246,79 +275,41 @@
     def ends(matrix):
         return z == root(matrix)
 
-    for piece in range(PIECES):
-        for matrix in range(3):
-            @pl.when(core != min(matrix, 1))
-            def _():
-                core_out[matrix, part(piece)] = total[matrix, part(piece)].astype(BF16)
-                core_copy(matrix, piece).start()
+    for matrices in ((0, 1), (2,)):
+        for piece in range(PIECES):
+            for matrix in matrices:
+                @pl.when(core != matrix % 2)
+                def _():
+                    core_out[matrix, part(piece)] = total[matrix, part(piece)].astype(BF16)
+                    core_copy(matrix, piece).start()
 
     for turn in range(1, heads):
         query_copy(turn).start()
 
     if attn:
-        def halo_copy(which):
-            source = (attn_k, attn_v)[which]
+        def halo_copy(which, relayed):
+            source = (attn_k, attn_v)[which].at[pl.ds(rows - WINDOW, WINDOW)]
+            if relayed:
+                source = relay.at[which]
             target = (key_window, value_window)[which]
-            return remote(source.at[pl.ds(rows - WINDOW, WINDOW)], target.at[pl.ds(0, WINDOW)],
-                          halo_s.at[which], halo_r.at[which], me + 1)
-
-        @pl.when(me < ctx - 1)
-        def _():
-            halo_copy(0).start()
-            halo_copy(1).start()
+            return remote(source, target.at[pl.ds(0, WINDOW)],
+                          halo_s.at[which], halo_r.at[which], halo_to)
+
+        @pl.when(jnp.logical_not(last))
+        def _():
+            halo_copy(0, False).start()
+            halo_copy(1, False).start()
+
+        @pl.when(relay_comes)
+        def _():
+            for which in range(2):
+                relay_copy(which).wait_recv()
+                halo_copy(which, True).start()
 
         @pl.when(me == 0)
         def _():
             key_window[0:WINDOW] = jnp.zeros((WINDOW, model), BF16)
             value_window[0:WINDOW] = jnp.zeros((WINDOW, model), BF16)
-
-    def sum_piece(matrix, piece, has_input):
-        core_copy(matrix, piece).wait_recv()
-        summed = total[matrix, part(piece)] + core_in[matrix, part(piece)].astype(F32)
-        if has_input:
-            chain_copy(matrix, piece).wait_recv()
-            summed = summed + chain_in[matrix, part(piece)].astype(F32)
-
-        @pl.when(ends(matrix))
-        def _():
-            total[matrix, part(piece)] = summed
-
-        @pl.when(jnp.logical_not(ends(matrix)))
-        def _():
-            chain_out[matrix, part(piece)] = summed.astype(BF16)
-            chain_copy(matrix, piece).start()
-
-    def start_chain(matrix, carry):
-        @pl.when((core == home(matrix)) & starts(matrix))
-        def _():
-            for piece in range(PIECES):
-                sum_piece(matrix, piece, False)
-        return carry
-
-    lax.fori_loop(0, 3, start_chain, 0)
-
-    order = [(0, 0)]
-    for piece in range(1, PIECES):
-        order += [(0, piece), (1, piece - 1)]
-    order += [(1, PIECES - 1)]
-
-    def sum_rest(matrix, piece):
-        @pl.when(jnp.logical_not(starts(matrix)))
-        def _():
-            sum_piece(matrix, piece, True)
-
-    @pl.when(core == 0)
-    def _():
-        for piece in range(PIECES):
-            sum_rest(0, piece)
-
-    near_sum = jnp.where(2 * z < chain, 1, 2)
-
-    @pl.when(core == 1)
-    def _():
-        for which, piece in order:
-            sum_rest(near_sum if which == 0 else 3 - near_sum, piece)
 
     half = min(256, width)
     tiles = width // half
@@ -365,61 +356,102 @@
 
         side_copy(matrix, piece).start()
 
-    def renew_here(matrix, carry):
-        @pl.when((core == home(matrix)) & ends(matrix))
-        def _():
-            renew(matrix)
+    def sum_piece(matrix, piece, behind):
+        here = part(piece)
+        core_copy(matrix, piece).wait_recv()
+        total[matrix, here] += core_in[matrix, here].astype(F32)
+
+        @pl.when(jnp.logical_not(starts(matrix)))
+        def _():
+            chain_copy(matrix, piece).wait_recv()
+            total[matrix, here] += chain_in[matrix, here].astype(F32)
+
+        @pl.when(jnp.logical_not(ends(matrix)))
+        def _():
+            chain_out[matrix, here] = total[matrix, here].astype(BF16)
+
+            @pl.when(behind)
+            def _():
+                chain_copy(0, piece).wait_send()
+
+            chain_copy(matrix, piece).start()
+
+    def sum_and_renew(turn, carry):
+        matrix = jnp.where(core == 0, 2 * turn, 1)
+
+        @pl.when((core == 0) | (turn == 0))
+        def _():
             for piece in range(PIECES):
-                pass_on(matrix, piece)
+                sum_piece(matrix, piece, turn == 1)
+
+            @pl.when(ends(matrix))
+            def _():
+                renew(matrix)
+                for piece in range(PIECES):
+                    pass_on(matrix, piece)
         return carry
 
-    lax.fori_loop(0, 3, renew_here, 0)
-
-    if attn:
-        @pl.when(me > 0)
-        def _():
-            halo_copy(0).wait_recv()
-            halo_copy(1).wait_recv()
-        attend(0)
-
-    def forward(matrix, piece):
-        @pl.when(jnp.logical_not(ends(matrix)))
+    lax.fori_loop(0, 2, sum_and_renew, 0)
+
+    def take(matrix, piece):
+        @pl.when((core == matrix % 2) & jnp.logical_not(ends(matrix)))
         def _():
             cast_copy(matrix, piece).wait_recv()
             pass_on(matrix, piece)
 
+        @pl.when(core != matrix % 2)
+        def _():
+            side_copy(matrix, piece).wait_recv()
+
     @pl.when(core == 0)
     def _():
-        for piece in range(PIECES):
-            forward(0, piece)
+        for matrix in (0, 1):
+            for piece in range(PIECES):
+                take(matrix, piece)
 
     @pl.when(core == 1)
     def _():
-        for which, piece in order:
-            forward(3 - near_sum if which == 0 else near_sum, piece)
-
-    for matrix in range(3):
-        @pl.when(core != min(matrix, 1))
-        def _():
+        for matrix in (1, 0):
             for piece in range(PIECES):
-                side_copy(matrix, piece).wait_recv()
-
-    def answer(query_ref):
-        query_rows = query_ref[...]
+                take(matrix, piece)
+
+    def hide(turn, carry):
+        query_rows = queries[flip(head, turn, heads)]
         pre_gate = mat(query_rows, renewed[0])
         pre_up = mat(query_rows, renewed[1])
-        hidden = (pre_gate * sigmoid(pre_gate) * pre_up).astype(BF16)
-        return mat(hidden, renewed[2]).astype(BF16)
-
-    def answer_turn(turn, carry):
+        hiddens[turn] = (pre_gate * sigmoid(pre_gate) * pre_up).astype(BF16)
+        return carry
+
+    def hide_turn(turn, carry):
         query_copy(turn).wait_recv()
-        answers[turn] = answer(queries.at[flip(head, turn, heads)])
-        answer_copy(turn).start()
-        return carry
-
-    lax.fori_loop(1, heads, answer_turn, 0)
+        return hide(turn, carry)
+
+    middle = (heads + 2) // 2
+    lax.fori_loop(1, middle, hide_turn, 0)
+    for piece in range(PIECES):
+        take(2, piece)
+        if piece == 0:
+            lax.fori_loop(middle, heads, hide_turn, 0)
+        if 2 * (piece + 1) % PIECES == 0:
+            part_index = 2 * (piece + 1) // PIECES - 1
+
+            def answer_turn(turn, carry):
+                cols = half_columns(part_index)
+                answers[turn, :, cols] = mat(hiddens[turn], renewed[2, :, cols]).astype(BF16)
+                answer_copy(turn, part_index).start()
+                return carry
+
+            lax.fori_loop(1, heads, answer_turn, 0)
     local[6].wait()
-    answers[0] = answer(queries.at[head])
+    hide(0, 0)
+    answers[0] = mat(hiddens[0], renewed[2]).astype(BF16)
+
+    if attn:
+        @pl.when(halo_comes)
+        def _():
+            halo_copy(0, False).wait_recv()
+            halo_copy(1, False).wait_recv()
+        attend(0)
 
     def finish(value, index):
         if attn:
@@ -428,7 +460,8 @@
 
     finish(answers[0], head)
     for turn in range(1, heads):
-        answer_copy(turn).wait_recv()
+        for part_index in range(2):
+            answer_copy(turn, part_index).wait_recv()
         other = flip(head, turn, heads)
         finish(returned[other], other)
 
@@ -436,27 +469,34 @@
         key_copy(turn).wait_send()
         og_copy(turn).wait_send()
         query_copy(turn).wait_send()
-        answer_copy(turn).wait_send()
-    if attn:
-        @pl.when(me < ctx - 1)
-        def _():
-            halo_copy(0).wait_send()
-            halo_copy(1).wait_send()
+        for part_index in range(2):
+            answer_copy(turn, part_index).wait_send()
+    if attn:
+        @pl.when(halo_sends)
+        def _():
+            halo_copy(0, False).wait_send()
+            halo_copy(1, False).wait_send()
+
+        @pl.when(relay_sends)
+        def _():
+            relay_copy(0).wait_send()
+            relay_copy(1).wait_send()
     for matrix in range(3):
-        @pl.when(core != min(matrix, 1))
+        @pl.when(core != matrix % 2)
         def _():
             for piece in range(PIECES):
                 core_copy(matrix, piece).wait_send()
 
-        @pl.when(core == min(matrix, 1))
+        @pl.when(core == matrix % 2)
         def _():
             for piece in range(PIECES):
                 side_copy(matrix, piece).wait_send()
 
-            @pl.when(jnp.logical_not(ends(matrix)))
-            def _():
-                for piece in range(PIECES):
-                    chain_copy(matrix, piece).wait_send()
+            if matrix > 0:
+                @pl.when(jnp.logical_not(ends(matrix)))
+                def _():
+                    for piece in range(PIECES):
+                        chain_copy(matrix, piece).wait_send()
 
             @pl.when(jnp.logical_not(starts(matrix)))
             def _():
@@ -465,6 +505,7 @@
 
 
 def memory_call(attn, *arrays):
+    arrays = arrays[:3] + (arrays[3].T,) + arrays[4:]
     rows = arrays[0].shape[0]
     heads, width = arrays[4].shape[:2]
     ctx = lax.axis_size("ctx")
@@ -474,10 +515,10 @@
     square = (width, width)
     tokens = (heads, rows, width)
     dma = pltpu.SemaphoreType.DMA
-    scratch = [pltpu.VMEM(tokens, BF16)] * 6
+    scratch = [pltpu.VMEM(tokens, BF16)] * 7
     scratch += [
         pltpu.VMEM((rows, model), BF16),
-        pltpu.VMEM((rows, heads), F32),
+        pltpu.VMEM((heads, rows), F32),
         pltpu.VMEM((3,) + square, BF16),
         pltpu.VMEM((3,) + square, BF16),
         pltpu.VMEM((3,) + square, F32),
@@ -485,7 +526,8 @@
     scratch += [pltpu.VMEM((3,) + square, BF16)] * 4
     scratch += [pltpu.VMEM(square, BF16)] * 4
     scratch += [dma((10,))]
-    scratch += [dma((heads,))] * 8
+    scratch += [dma((heads,))] * 6
+    scratch += [dma((heads, 2))] * 2
     scratch += [dma((3, PIECES))] * 8
     if attn:
         scratch += [
@@ -493,9 +535,9 @@
             pltpu.VMEM((rows + WINDOW, swa_model), BF16),
             pltpu.VMEM((rows + WINDOW, swa_model), BF16),
             pltpu.VMEM((rows, swa_model), F32),
-            dma((2,)),
-            dma((2,)),
+            pltpu.VMEM((2, WINDOW, swa_model), BF16),
         ]
+        scratch += [dma((2,))] * 4
     sizes = (ctx, heads, chain, rows, width, swa_model, attn)
     flops = 2 * rows * heads * width * width * 9 + 6 * NS_ITERS * width**3
     return pl.pallas_call(
@@ -508,7 +550,7 @@
             flops=flops, bytes_accessed=8 * rows * model * 2, transcendentals=rows * model
         ),
         compiler_params=pltpu.CompilerParams(
-            collective_id=0, has_side_effects=True, vmem_limit_bytes=50 * 1024 * 1024
+            collective_id=0, has_side_effects=True, vmem_limit_bytes=60 * 1024 * 1024
         ),
     )(*arrays)
 

time: 101 us -> 88.6 us (0.88)
  Pallas kernels: 96.2 us -> 86.1 us
  local copies, waits for them, and re-layouts: 4.23 us -> 2.3 us
    pallas_call x1, Pallas kernels: 96.2 us -> 86.1 us  [memory_call(): pl.pallas_call(functools.partial(kernel, sizes), out_shape=jax.ShapeDtype...]
    unnamed x6 -> x1, local copies, waits for them, and re-layouts: 4.23 us -> 2.3 us
where the time goes in v2:
time: 88.6 us; the launch traced here: 88.4 us
  Pallas kernels  86.1 us (97%)
  local copies, waits for them, and re-layouts  2.3 us (3%)
    pallas_call x1, Pallas kernels, memory_call(): pl.pallas_call(functools.partial(kernel, sizes), out_shape=jax.ShapeDtype...  86.1 us
    unnamed x1, local copies, waits for them, and re-layouts  2.3 us

profile of v2, /device:TPU:25, one launch (start us, length us, event | category | flops | bytes accessed | tf_op | source)
XLA Modules:
  0.0 88.4 jit_solution(12191420124778071521)
XLA Ops:
  0.0 86.1 %shard_map.100 = bf16[256,2048]{1,0:T(8,128)(2,1)} custom-call(bf16[256,2048]{1,0:T(8,128)(2,1)} %refs_0_.1, bf16[256,2048]{1,0:T(8,128)(2,1)} %refs_1_.1, bf16[256,2048]{1,0:T(8,128)(2,1)} %refs_2_.1, f32[4,256]{1,0:T(4,128)} %bitcast.1, bf16[4,512,512]{2,1,0:T(8,128)(2,1)} %refs_4_.1, bf16[4,512,512]{2,1,0:T(8,128)(2,1)} %refs_5_.1, ...), custom_call_target="tpu_custom_call" | custom-call | flops 6442450944 | bytes 8388608 | tf_op jit(solution)/shard_map/pallas_call | solution.py:543
  86.1 2.3 %copy.12 = bf16[256,2048]{1,0:T(8,128)(2,1)} copy(bf16[256,2048]{1,0:T(8,128)(2,1)} %shard_map.100) | data formatting | bytes 2097152

commit v3 on v2

--- a/solution.py
+++ b/solution.py
@@ -11,7 +11,7 @@
 SWA_DH = 128
 WINDOW = 128
 NS_ITERS = 2
-PIECES = 4
+PIECES = 8
 
 linear_coef = 3.4445
 square_coef = -4.775
@@ -174,7 +174,7 @@
     for turn in range(1, heads):
         og_copy(turn).start()
 
-    def accumulate(key_ref, og_ref, first):
+    def accumulate(key_ref, og_ref, first, done=None):
         key_rows = key_ref[...]
         og = og_ref[...]
         pre_gate = mat(key_rows, weights[0])
@@ -182,9 +182,9 @@
         hidden_grad = mat_tb(og, weights[2])
         sig = sigmoid(pre_gate)
         activated = pre_gate * sig
-        hidden = (activated * pre_up).astype(BF16)
         gate_grad = (hidden_grad * pre_up * (sig * (1.0 + pre_gate * (1.0 - sig)))).astype(BF16)
         up_grad = (hidden_grad * activated).astype(BF16)
+        hidden = (activated * pre_up).astype(BF16)
         for index, (left, right) in enumerate(
             ((key_rows, gate_grad), (key_rows, up_grad), (hidden, og))
         ):
@@ -192,6 +192,8 @@
                 total[index] = mat_ta(left, right)
             else:
                 total[index] += mat_ta(left, right)
+            if done is not None:
+                done(index)
 
     for index in range(2, 6):
         local[index].wait()
@@ -227,18 +229,6 @@
         for block in range(1, rows // WINDOW):
             attend(block)
 
-    def gather_turn(turn, carry):
-        key_copy(turn).wait_recv()
-        og_copy(turn).wait_recv()
-        other = flip(head, turn, heads)
-        accumulate(keys.at[other], grads.at[other], False)
-        return carry
-
-    lax.fori_loop(1, heads, gather_turn, 0)
-
-    def home(matrix):
-        return lax.rem(matrix, 2)
-
     def root(matrix):
         return jnp.where(matrix == 1, chain - 1, 0)
 
@@ -257,16 +247,18 @@
                       chain_s.at[matrix, piece], chain_r.at[matrix, piece],
                       me + step * toward(matrix))
 
-    def piece_columns(piece):
-        return pl.ds(piece * piece_rows, piece_rows)
+    def block(matrix, piece):
+        half = width // 2
+        cols = 2 * width // PIECES
+        return renewed.at[matrix, pl.ds(piece % 2 * half, half), pl.ds(piece // 2 * cols, cols)]
 
     def cast_copy(matrix, piece):
-        here = renewed.at[matrix, :, piece_columns(piece)]
+        here = block(matrix, piece)
         return remote(here, here, cast_s.at[matrix, piece], cast_r.at[matrix, piece],
                       me - step * toward(matrix))
 
     def side_copy(matrix, piece):
-        here = renewed.at[matrix, :, piece_columns(piece)]
+        here = block(matrix, piece)
         return remote(here, here, side_s.at[matrix, piece], side_r.at[matrix, piece], mate)
 
     def starts(matrix):
@@ -275,13 +267,26 @@
     def ends(matrix):
         return z == root(matrix)
 
-    for matrices in ((0, 1), (2,)):
-        for piece in range(PIECES):
-            for matrix in matrices:
-                @pl.when(core != matrix % 2)
-                def _():
-                    core_out[matrix, part(piece)] = total[matrix, part(piece)].astype(BF16)
-                    core_copy(matrix, piece).start()
+    def exchange(matrix):
+        @pl.when(core != matrix % 2)
+        def _():
+            for piece in range(PIECES):
+                core_out[matrix, part(piece)] = total[matrix, part(piece)].astype(BF16)
+                core_copy(matrix, piece).start()
+
+    def gather_turn(turn, carry, done=None):
+        key_copy(turn).wait_recv()
+        og_copy(turn).wait_recv()
+        other = flip(head, turn, heads)
+        accumulate(keys.at[other], grads.at[other], False, done)
+        return carry
+
+    if heads > 1:
+        lax.fori_loop(1, heads - 1, gather_turn, 0)
+        gather_turn(heads - 1, 0, exchange)
+    else:
+        for matrix in range(3):
+            exchange(matrix)
 
     for turn in range(1, heads):
         query_copy(turn).start()
@@ -311,37 +316,18 @@
             key_window[0:WINDOW] = jnp.zeros((WINDOW, model), BF16)
             value_window[0:WINDOW] = jnp.zeros((WINDOW, model), BF16)
 
-    half = min(256, width)
-    tiles = width // half
-
-    def tile_loop(body):
-        def run(index, carry):
-            body(pl.ds(pl.multiple_of(index * half, half), half))
-            return carry
-        lax.fori_loop(0, tiles, run, 0)
-
     def renew(matrix):
         gradient = total[matrix]
         norm = jnp.sqrt(jnp.sum(gradient * gradient) + epsilon)
-        iter_a[...] = (gradient / norm).astype(BF16)
+        iter_a[...] = (gradient * (1.0 / norm)).astype(BF16)
         source, target = iter_a, iter_b
         for _ in range(NS_ITERS):
-            def gram_rows(here, source=source):
-                gram[here, :] = mat_tb(source[here, :], source[...]).astype(BF16)
-
-            def poly_rows(here):
-                mine = gram[here, :]
-                square = mat(mine, gram[...])
-                poly[here, :] = (square_coef * mine.astype(F32) + quartic_coef * square).astype(BF16)
-
-            def next_rows(here, source=source, target=target):
-                target[here, :] = (
-                    linear_coef * source[here, :].astype(F32) + mat(poly[here, :], source[...])
-                ).astype(BF16)
-
-            tile_loop(gram_rows)
-            tile_loop(poly_rows)
-            tile_loop(next_rows)
+            gram[...] = mat_tb(source[...], source[...]).astype(BF16)
+            square = mat(gram[...], gram[...])
+            poly[...] = (square_coef * gram[...].astype(F32) + quartic_coef * square).astype(BF16)
+            target[...] = (
+                linear_coef * source[...].astype(F32) + mat(poly[...], source[...])
+            ).astype(BF16)
             source, target = target, source
         initial = weights[matrix].astype(F32)
         stepped = initial - source[...].astype(F32)

time: 88.6 us -> 84.5 us (0.954)
  Pallas kernels: 86.1 us -> 82.1 us
    pallas_call x1, Pallas kernels: 86.1 us -> 82.1 us  [memory_call(): pl.pallas_call(functools.partial(kernel, sizes), out_shape=jax.ShapeDtype...]
where the time goes in v3:
time: 84.5 us; the launch traced here: 84.4 us
  Pallas kernels  82.1 us (97%)
  local copies, waits for them, and re-layouts  2.3 us (3%)
    pallas_call x1, Pallas kernels, memory_call(): pl.pallas_call(functools.partial(kernel, sizes), out_shape=jax.ShapeDtype...  82.1 us
    unnamed x1, local copies, waits for them, and re-layouts  2.3 us

profile of v3, /device:TPU:25, one launch (start us, length us, event | category | flops | bytes accessed | tf_op | source)
XLA Modules:
  0.0 84.4 jit_solution(4843727125437404192)
XLA Ops:
  0.0 82.1 %shard_map.100 = bf16[256,2048]{1,0:T(8,128)(2,1)} custom-call(bf16[256,2048]{1,0:T(8,128)(2,1)} %refs_0_.1, bf16[256,2048]{1,0:T(8,128)(2,1)} %refs_1_.1, bf16[256,2048]{1,0:T(8,128)(2,1)} %refs_2_.1, f32[4,256]{1,0:T(4,128)} %bitcast.1, bf16[4,512,512]{2,1,0:T(8,128)(2,1)} %refs_4_.1, bf16[4,512,512]{2,1,0:T(8,128)(2,1)} %refs_5_.1, ...), custom_call_target="tpu_custom_call" | custom-call | flops 6442450944 | bytes 8388608 | tf_op jit(solution)/shard_map/pallas_call | solution.py:529
  82.1 2.3 %copy.12 = bf16[256,2048]{1,0:T(8,128)(2,1)} copy(bf16[256,2048]{1,0:T(8,128)(2,1)} %shard_map.100) | data formatting | bytes 2097152

commit v4 on v3

--- a/solution.py
+++ b/solution.py
@@ -412,22 +412,37 @@
         query_copy(turn).wait_recv()
         return hide(turn, carry)
 
-    middle = (heads + 2) // 2
-    lax.fori_loop(1, middle, hide_turn, 0)
-    for piece in range(PIECES):
-        take(2, piece)
-        if piece == 0:
-            lax.fori_loop(middle, heads, hide_turn, 0)
-        if 2 * (piece + 1) % PIECES == 0:
-            part_index = 2 * (piece + 1) // PIECES - 1
-
-            def answer_turn(turn, carry):
-                cols = half_columns(part_index)
-                answers[turn, :, cols] = mat(hiddens[turn], renewed[2, :, cols]).astype(BF16)
-                answer_copy(turn, part_index).start()
-                return carry
-
-            lax.fori_loop(1, heads, answer_turn, 0)
+    def answer_half(part_index):
+        def answer_turn(turn, carry):
+            cols = half_columns(part_index)
+            answers[turn, :, cols] = mat(hiddens[turn], renewed[2, :, cols]).astype(BF16)
+            answer_copy(turn, part_index).start()
+            return carry
+
+        lax.fori_loop(1, heads, answer_turn, 0)
+
+    hands_on = (core == 0) & jnp.logical_not(starts(2) | ends(2))
+
+    @pl.when(hands_on)
+    def _():
+        turn = 1
+        for piece in range(PIECES):
+            take(2, piece)
+            if piece % 2 == 1 and turn < heads:
+                hide_turn(turn, 0)
+                turn += 1
+        lax.fori_loop(turn, heads, hide_turn, 0)
+        answer_half(0)
+        answer_half(1)
+
+    @pl.when(jnp.logical_not(hands_on))
+    def _():
+        lax.fori_loop(1, heads, hide_turn, 0)
+        for piece in range(PIECES):
+            take(2, piece)
+            if 2 * (piece + 1) % PIECES == 0:
+                answer_half(2 * (piece + 1) // PIECES - 1)
+
     local[6].wait()
     hide(0, 0)
     answers[0] = mat(hiddens[0], renewed[2]).astype(BF16)
@@ -536,7 +551,7 @@
             flops=flops, bytes_accessed=8 * rows * model * 2, transcendentals=rows * model
         ),
         compiler_params=pltpu.CompilerParams(
-            collective_id=0, has_side_effects=True, vmem_limit_bytes=60 * 1024 * 1024
+            collective_id=0, has_side_effects=True, vmem_limit_bytes=52 * 1024 * 1024
         ),
     )(*arrays)
 

time: 84.5 us -> 82.5 us (0.976)
  Pallas kernels: 82.1 us -> 80.6 us
    pallas_call x1, Pallas kernels: 82.1 us -> 80.6 us  [memory_call(): pl.pallas_call(functools.partial(kernel, sizes), out_shape=jax.ShapeDtype...]
    unnamed x1 -> x3, local copies, waits for them, and re-layouts: 2.3 us -> 1.66 us
where the time goes in v4:
time: 82.5 us; the launch traced here: 82.3 us
  Pallas kernels  80.6 us (98%)
  local copies, waits for them, and re-layouts  1.66 us (2%)
    pallas_call x1, Pallas kernels, memory_call(): pl.pallas_call(functools.partial(kernel, sizes), out_shape=jax.ShapeDtype...  80.6 us
    unnamed x3, local copies, waits for them, and re-layouts  1.66 us

profile of v4, /device:TPU:25, one launch (start us, length us, event | category | flops | bytes accessed | tf_op | source)
XLA Modules:
  0.0 82.3 jit_solution(12648779897722383418)
XLA Ops:
  0.0 0.0 copy-start
  0.0 0.7 copy-done
  0.7 80.6 %shard_map.100 = bf16[256,2048]{1,0:T(8,128)(2,1)S(1)} custom-call(bf16[256,2048]{1,0:T(8,128)(2,1)} %refs_0_.1, bf16[256,2048]{1,0:T(8,128)(2,1)} %refs_1_.1, bf16[256,2048]{1,0:T(8,128)(2,1)} %refs_2_.1, f32[4,256]{1,0:T(4,128)S(1)} %bitcast.1, bf16[4,512,512]{2,1,0:T(8,128)(2,1)} %refs_4_.1, bf16[4,512,512]{2,1,0:T(8,128)(2,1)} %refs_5_.1, ...), custom_call_target="tpu_custom_call" | custom-call | flops 6442450944 | bytes 8388608 | tf_op jit(solution)/shard_map/pallas_call | solution.py:544
  81.3 1.0 %copy.12 = bf16[256,2048]{1,0:T(8,128)(2,1)} copy(bf16[256,2048]{1,0:T(8,128)(2,1)S(1)} %shard_map.100) | data formatting | bytes 2097152
Async XLA Ops:
  0.0 0.7 copy-start

commit v5 on v4

--- a/solution.py
+++ b/solution.py
@@ -57,12 +57,12 @@
         attn_q, attn_k, attn_v = refs[:3]
         refs = refs[3:]
     out = refs[0]
-    (keys, grads, queries, grad_out, answers, returned, hiddens, values, rates, weights, renewed,
+    (keys, grads, queries, grad_out, answers, returned, hiddens, gates, ups, values, rates, weights, renewed,
      total, core_out, core_in, chain_out, chain_in, iter_a, iter_b, gram, poly,
      local_sem, key_s, key_r, og_s, og_r, q_s, q_r, ans_s, ans_r,
-     core_s, core_r, chain_s, chain_r, cast_s, cast_r, side_s, side_r) = refs[1:38]
-    if attn:
-        q_rows, key_window, value_window, attended, relay, halo_s, halo_r, relay_s, relay_r = refs[38:]
+     core_s, core_r, chain_s, chain_r, cast_s, cast_r, side_s, side_r) = refs[1:40]
+    if attn:
+        q_rows, key_window, value_window, attended, relay, halo_s, halo_r, relay_s, relay_r = refs[40:]
 
     me = lax.axis_index("ctx")
     core = lax.rem(me, 2)
@@ -171,14 +171,19 @@
         grad_out[index] = (
             -(rate_columns[:, index : index + 1] * values[:, cols].astype(F32))
         ).astype(BF16)
-    for turn in range(1, heads):
+    for turn in range(1, heads - 1):
         og_copy(turn).start()
 
-    def accumulate(key_ref, og_ref, first, done=None):
+    def pre_products(turn, key_ref):
+        key_rows = key_ref[...]
+        gates[turn] = mat(key_rows, weights[0])
+        ups[turn] = mat(key_rows, weights[1])
+
+    def accumulate(turn, key_ref, og_ref, first, done=None):
         key_rows = key_ref[...]
         og = og_ref[...]
-        pre_gate = mat(key_rows, weights[0])
-        pre_up = mat(key_rows, weights[1])
+        pre_gate = gates[turn]
+        pre_up = ups[turn]
         hidden_grad = mat_tb(og, weights[2])
         sig = sigmoid(pre_gate)
         activated = pre_gate * sig
@@ -197,7 +202,8 @@
 
     for index in range(2, 6):
         local[index].wait()
-    accumulate(keys.at[head], grad_out.at[head], True)
+    pre_products(0, keys.at[head])
+    accumulate(0, keys.at[head], grad_out.at[head], True)
 
     if attn:
         score_scale = 1.0 / math.sqrt(SWA_DH)
@@ -274,14 +280,24 @@
                 core_out[matrix, part(piece)] = total[matrix, part(piece)].astype(BF16)
                 core_copy(matrix, piece).start()
 
+    def key_turn(turn, carry):
+        key_copy(turn).wait_recv()
+
+        @pl.when(turn == heads - 1)
+        def _():
+            og_copy(turn).start()
+
+        pre_products(turn, keys.at[flip(head, turn, heads)])
+        return carry
+
     def gather_turn(turn, carry, done=None):
-        key_copy(turn).wait_recv()
         og_copy(turn).wait_recv()
         other = flip(head, turn, heads)
-        accumulate(keys.at[other], grads.at[other], False, done)
+        accumulate(turn, keys.at[other], grads.at[other], False, done)
         return carry
 
     if heads > 1:
+        lax.fori_loop(1, heads, key_turn, 0)
         lax.fori_loop(1, heads - 1, gather_turn, 0)
         gather_turn(heads - 1, 0, exchange)
     else:
@@ -516,7 +532,7 @@
     square = (width, width)
     tokens = (heads, rows, width)
     dma = pltpu.SemaphoreType.DMA
-    scratch = [pltpu.VMEM(tokens, BF16)] * 7
+    scratch = [pltpu.VMEM(tokens, BF16)] * 7 + [pltpu.VMEM(tokens, F32)] * 2
     scratch += [
         pltpu.VMEM((rows, model), BF16),
         pltpu.VMEM((heads, rows), F32),

time: 82.5 us -> 82.3 us (level)
  no operation moved by 1% of the time
where the time goes in v5:
time: 82.3 us; the launch traced here: 82.1 us
  Pallas kernels  80.5 us (98%)
  local copies, waits for them, and re-layouts  1.66 us (2%)
    pallas_call x1, Pallas kernels, memory_call(): pl.pallas_call(functools.partial(kernel, sizes), out_shape=jax.ShapeDtype...  80.5 us
    unnamed x3, local copies, waits for them, and re-layouts  1.66 us

profile of v5, /device:TPU:25, one launch (start us, length us, event | category | flops | bytes accessed | tf_op | source)
XLA Modules:
  0.0 82.1 jit_solution(10816144915105457197)
XLA Ops:
  0.0 0.0 copy-start
  0.0 0.7 copy-done
  0.7 80.5 %shard_map.100 = bf16[256,2048]{1,0:T(8,128)(2,1)S(1)} custom-call(bf16[256,2048]{1,0:T(8,128)(2,1)} %refs_0_.1, bf16[256,2048]{1,0:T(8,128)(2,1)} %refs_1_.1, bf16[256,2048]{1,0:T(8,128)(2,1)} %refs_2_.1, f32[4,256]{1,0:T(4,128)S(1)} %bitcast.1, bf16[4,512,512]{2,1,0:T(8,128)(2,1)} %refs_4_.1, bf16[4,512,512]{2,1,0:T(8,128)(2,1)} %refs_5_.1, ...), custom_call_target="tpu_custom_call" | custom-call | flops 6442450944 | bytes 8388608 | tf_op jit(solution)/shard_map/pallas_call | solution.py:560
  81.2 1.0 %copy.12 = bf16[256,2048]{1,0:T(8,128)(2,1)} copy(bf16[256,2048]{1,0:T(8,128)(2,1)S(1)} %shard_map.100) | data formatting | bytes 2097152
Async XLA Ops:
  0.0 0.7 copy-start

commit v6 on v5

--- a/solution.py
+++ b/solution.py
@@ -224,7 +224,7 @@
                 masked = jnp.where(allowed, scores, -jnp.inf)
                 peak = jnp.max(masked, axis=-1, keepdims=True)
                 exponent = jnp.exp(masked - peak)
-                probs = (exponent / jnp.sum(exponent, axis=-1, keepdims=True)).astype(BF16)
+                probs = (exponent * (1.0 / jnp.sum(exponent, axis=-1, keepdims=True))).astype(BF16)
                 attended[here, cols] = mat(probs, value_window[there, cols])
                 return carry
 

time: 82.3 us -> 82.3 us (level)
  no operation moved by 1% of the time
where the time goes in v6:
time: 82.3 us; the launch traced here: 82.1 us
  Pallas kernels  80.5 us (98%)
  local copies, waits for them, and re-layouts  1.66 us (2%)
    pallas_call x1, Pallas kernels, memory_call(): pl.pallas_call(functools.partial(kernel, sizes), out_shape=jax.ShapeDtype...  80.5 us
    unnamed x3, local copies, waits for them, and re-layouts  1.66 us

profile of v6, /device:TPU:25, one launch (start us, length us, event | category | flops | bytes accessed | tf_op | source)
XLA Modules:
  0.0 82.1 jit_solution(10816144915105457197)
XLA Ops:
  0.0 0.0 copy-start
  0.0 0.7 copy-done
  0.7 80.5 %shard_map.100 = bf16[256,2048]{1,0:T(8,128)(2,1)S(1)} custom-call(bf16[256,2048]{1,0:T(8,128)(2,1)} %refs_0_.1, bf16[256,2048]{1,0:T(8,128)(2,1)} %refs_1_.1, bf16[256,2048]{1,0:T(8,128)(2,1)} %refs_2_.1, f32[4,256]{1,0:T(4,128)S(1)} %bitcast.1, bf16[4,512,512]{2,1,0:T(8,128)(2,1)} %refs_4_.1, bf16[4,512,512]{2,1,0:T(8,128)(2,1)} %refs_5_.1, ...), custom_call_target="tpu_custom_call" | custom-call | flops 6442450944 | bytes 8388608 | tf_op jit(solution)/shard_map/pallas_call | solution.py:560
  81.2 1.0 %copy.12 = bf16[256,2048]{1,0:T(8,128)(2,1)} copy(bf16[256,2048]{1,0:T(8,128)(2,1)S(1)} %shard_map.100) | data formatting | bytes 2097152
Async XLA Ops:
  0.0 0.7 copy-start
